TPU v7x, 512 devices: a whole 4x8x8 slice. The times are simulated.
512 devices in a mesh: span: 16 (over x, z_hi, core), seq: 32 (over z_lo, y).
Axes of the slice: x: 4, y: 8, z: 8 (z_hi: 2, z_lo: 4; z = z_hi * 4 + z_lo), core: 2. Of those that a mesh axis runs over, the one named last changes fastest.
Arguments:
- queries: bfloat16 [16, 768, 4096], P('span', 'seq'), may hold values from -160 to 160
- keys: bfloat16 [16, 768, 4096], P('span', 'seq'), may hold values from -5 to 5
- values: bfloat16 [16, 768, 4096], P('span', 'seq'), may hold values from -6 to 6
- step_index: int32 [16], replicated, may hold values from 0 to 15
- frame_counts: int32 [16], replicated, may hold values from 1 to 8
- frame_layout: int32 [8, 8], replicated, may hold values 0 or 1
- gate_table: float32 [16, 4096], replicated, may hold values from -8 to 8
Outputs:
- mixed: bfloat16 [16, 768, 4096], P('span', 'seq')
All inputs are finite; a program needn't handle non-finite values.
Results may differ from a plain program's by a relative error of at most 0.0075.
Values may be sent and summed in bfloat16 or wider, within the bound.
A program may use at most 64 MiB of HBM per device.

v0:
```python
import math

import jax
import jax.numpy as jnp
from jax import lax
from jax.sharding import PartitionSpec as P

HD = 128
FRAMES = 8


def fresh_state(head_count, row_count):
    return (
        jnp.full((head_count, row_count, 1), -1e30, jnp.float32),
        jnp.zeros((head_count, row_count, 1), jnp.float32),
        jnp.zeros((head_count, row_count, HD), jnp.float32),
    )


def attend_block(
    running,
    query_heads,
    query_first,
    query_span,
    key_block,
    key_first,
    is_live,
    counts,
    layout,
    span_rows,
    spans,
):

    def update():
        row_max, row_total, row_accum = running
        query_count = query_heads.shape[0]
        head_count = query_heads.shape[1]
        block_rows = key_block.shape[1]
        frame_tok = span_rows // FRAMES
        key_ids = key_first + jnp.arange(block_rows)
        key_span = key_ids // span_rows
        key_frame = key_ids % span_rows // frame_tok
        query_frame = (query_first + jnp.arange(query_count)) // frame_tok
        span_ids = jnp.arange(spans)
        key_count = jnp.sum(
            jnp.where(key_span[:, None] == span_ids[None, :], counts[None, :], 0), axis=1
        )
        own_count = jnp.sum(jnp.where(span_ids == query_span, counts, 0))
        frame_ids = jnp.arange(FRAMES)
        query_sel = (query_frame[:, None] == frame_ids[None, :]).astype(jnp.float32)
        key_sel = (key_frame[:, None] == frame_ids[None, :]).astype(jnp.float32)
        layout_rows = jnp.dot(
            query_sel, layout.astype(jnp.float32), precision=lax.Precision.HIGHEST
        )
        layout_hit = jnp.dot(layout_rows, key_sel.T, precision=lax.Precision.HIGHEST) > 0.5
        earlier = (key_span < query_span) & (key_frame < key_count)
        same_frame = query_frame[:, None] == key_frame[None, :]
        own_frames = (key_span == query_span)[None, :] & (
            (key_frame < own_count)[None, :] & layout_hit | same_frame
        )
        visible = (earlier[None, :] | own_frames)[None, :, :]
        key_part = key_block[0].reshape(block_rows, head_count, HD)
        value_part = key_block[1].reshape(block_rows, head_count, HD)
        scores = jnp.einsum(
            "qhd,khd->hqk", query_heads, key_part, preferred_element_type=jnp.float32
        ) / math.sqrt(HD)
        block_max = jnp.max(jnp.where(visible, scores, -1e30), axis=2, keepdims=True)
        new_max = jnp.maximum(row_max, block_max)
        exps = jnp.where(visible, jnp.exp(scores - new_max), 0.0)
        rescale = jnp.exp(row_max - new_max)
        new_total = row_total * rescale + jnp.sum(exps, axis=2, keepdims=True)
        summed = jnp.einsum(
            "hqk,khd->hqd",
            exps.astype(jnp.bfloat16),
            value_part,
            preferred_element_type=jnp.float32,
        )
        return (new_max, new_total, row_accum * rescale + summed)

    return lax.cond(is_live, update, lambda: running)


def over_portion(running, portion, apply_block, block_rows):
    total_rows = portion.shape[1]

    def one_turn(turn_index, carried):
        key_block = lax.dynamic_slice_in_dim(portion, turn_index * block_rows, block_rows, 1)
        return apply_block(carried, key_block, turn_index * block_rows)

    return lax.fori_loop(0, total_rows // block_rows, one_turn, running)


def finish(running):
    row_max, row_total, row_accum = running
    normal = (row_accum / row_total).astype(jnp.bfloat16)
    head_count, row_count, head_size = normal.shape
    return normal.transpose(1, 0, 2).reshape(row_count, head_count * head_size)


def shards(queries, keys, values, step_index, frame_counts, frame_layout, gate_table):
    span_id = lax.axis_index("span")
    spans = lax.axis_size("span")
    query_cols, key_cols, value_cols = (
        lax.all_to_all(queries, "seq", split_axis=2, concat_axis=1, tiled=True),
        lax.all_to_all(keys, "seq", split_axis=2, concat_axis=1, tiled=True),
        lax.all_to_all(values, "seq", split_axis=2, concat_axis=1, tiled=True),
    )
    span_rows = query_cols.shape[1]
    width = query_cols.shape[2]
    head_count = width // HD
    query_heads = query_cols[0].reshape(span_rows, head_count, HD)
    key_value = jnp.stack([key_cols[0], value_cols[0]])

    def for_queries(query_rows, query_first, query_span):

        def apply_block(running, key_block, key_first):
            is_live = key_first < (query_span + 1) * span_rows
            return attend_block(
                running,
                query_rows,
                query_first,
                query_span,
                key_block,
                key_first,
                is_live,
                frame_counts,
                frame_layout,
                span_rows,
                spans,
            )

        return apply_block

    apply_own = for_queries(query_heads, 0, span_id)
    running = over_portion(
        fresh_state(head_count, span_rows),
        lax.all_gather(key_value, "span", axis=1, tiled=True),
        apply_own,
        span_rows,
    )
    attended = finish(running)
    token_rows = lax.all_to_all(attended[None], "seq", split_axis=1, concat_axis=2, tiled=True)
    own_step = jnp.sum(jnp.where(jnp.arange(spans) == span_id, step_index, 0))
    picked = jnp.arange(gate_table.shape[0]) == own_step
    gate_row = jnp.sum(jnp.where(picked[:, None], gate_table, 0.0), axis=0)
    return (token_rows.astype(jnp.float32) * gate_row[None, None, :]).astype(jnp.bfloat16)


def solution(mesh):
    in_specs = (
        P("span", "seq", None),
        P("span", "seq", None),
        P("span", "seq", None),
        P(),
        P(),
        P(),
        P(),
    )
    out_specs = P("span", "seq", None)
    return jax.shard_map(shards, mesh=mesh, in_specs=in_specs, out_specs=out_specs, check_vma=False)
```

profile of v0, /device:TPU:271, one launch (start us, length us, event | category | flops | bytes accessed | tf_op | source)
XLA Modules:
  0.0 392.6 jit_solution(576642012464214609)
XLA Ops:
  6.5 4.4 %copy.66 = bf16[1,24,4096]{1,0,2:T(2,128)(2,1)S(1)} copy(bf16[1,24,4096]{2,1,0:T(8,128)(2,1)} %param.13) | data formatting | bytes 393216 | tf_op args[2]
  11.5 22.5 %reduce.13 = bf16[4096,24]{1,0:T(8,128)(2,1)S(1)} reduce(bf16[4096,1,24]{2,1,0:T(2,128)(2,1)S(1)} %bitcast.74, bf16[]{:T(256)} %broadcast.318), dimensions={1}, to_apply=%bitcast.59.reduce_sub_computation | reduce | bytes 393218
  34.0 2.1 reshape.179
  36.1 9.9 %all-to-all-start.1 = ((bf16[32,2,1536]{2,1,0:T(2,128)(2,1)}), bf16[32,2,1536]{2,1,0:T(2,128)(2,1)S(1)}, u32[]{:S(2)}, u32[]{:S(2)}) async-start(bf16[32,2,1536]{2,1,0:T(2,128)(2,1)} %reshape.179), calls=%async_computation.1 | async-start | bytes 393216 | tf_op jit(solution)/shard_map/all_to_all | solution.py:106
  46.0 2.8 copy.63
  48.7 22.5 %reduce.14 = bf16[4096,24]{1,0:T(8,128)(2,1)S(1)} reduce(bf16[4096,1,24]{2,1,0:T(2,128)(2,1)S(1)} %bitcast.78, bf16[]{:T(256)} %broadcast.318), dimensions={1}, to_apply=%bitcast.61.reduce_sub_computation | reduce | bytes 393218
  71.2 2.1 reshape.181
  73.3 9.6 %all-to-all-start = ((bf16[32,2,1536]{2,1,0:T(2,128)(2,1)}), bf16[32,2,1536]{2,1,0:T(2,128)(2,1)S(1)}, u32[]{:S(2)}, u32[]{:S(2)}) async-start(bf16[32,2,1536]{2,1,0:T(2,128)(2,1)} %reshape.181), calls=%async_computation | async-start | bytes 393216 | tf_op jit(solution)/shard_map/all_to_all | solution.py:105
  83.1 3.0 reshape.180
  86.1 2.1 copy.67
  88.4 4.1 %all-to-all-done = bf16[32,2,1536]{2,1,0:T(2,128)(2,1)S(1)} async-done(((bf16[32,2,1536]{2,1,0:T(2,128)(2,1)}), bf16[32,2,1536]{2,1,0:T(2,128)(2,1)S(1)}, u32[]{:S(2)}, u32[]{:S(2)}) %all-to-all-start) | async-done | bytes 196640 | tf_op jit(solution)/shard_map/all_to_all | solution.py:105
  92.4 3.0 reshape.182
  95.4 2.1 copy.64
  98.5 2.8 copy.69
  101.3 22.5 %reduce.15 = bf16[4096,24]{1,0:T(8,128)(2,1)S(1)} reduce(bf16[4096,1,24]{2,1,0:T(2,128)(2,1)S(1)} %bitcast.79, bf16[]{:T(256)} %broadcast.318), dimensions={1}, to_apply=%bitcast.63.reduce_sub_computation | reduce | bytes 393218
  123.7 2.1 reshape.183
  125.8 5.5 %all-to-all-start.2 = ((bf16[32,2,1536]{2,1,0:T(2,128)(2,1)}), bf16[32,2,1536]{2,1,0:T(2,128)(2,1)S(1)}, u32[]{:S(2)}, u32[]{:S(2)}) async-start(bf16[32,2,1536]{2,1,0:T(2,128)(2,1)} %reshape.183), calls=%async_computation.2 | async-start | bytes 393216 | tf_op jit(solution)/shard_map/all_to_all | solution.py:104
  131.4 9.6 %all-to-all-done.2 = bf16[32,2,1536]{2,1,0:T(2,128)(2,1)S(1)} async-done(((bf16[32,2,1536]{2,1,0:T(2,128)(2,1)}), bf16[32,2,1536]{2,1,0:T(2,128)(2,1)S(1)}, u32[]{:S(2)}, u32[]{:S(2)}) %all-to-all-start.2) | async-done | bytes 196640 | tf_op jit(solution)/shard_map/all_to_all | solution.py:104
  140.9 3.0 reshape.184
  143.9 2.1 copy.70
  146.2 34.2 %all-gather.2.cloned.1.call-done = bf16[2,12288,128]{2,1,0:T(8,128)(2,1)} async-done(((bf16[2,768,128]{2,1,0:T(8,128)(2,1)}), bf16[2,12288,128]{2,1,0:T(8,128)(2,1)}) %all-gather.2.cloned.1.call-update) | async-done | bytes 6291472 | tf_op jit(solution)/shard_map/all_gather | solution.py:137
  180.4 172.3 %while.19 = (s32[]{:T(128)}, f32[1,768,1]{1,2,0:T(1,128)S(1)}, f32[1,768,1]{1,2,0:T(1,128)S(1)}, f32[1,768,128]{2,1,0:T(8,128)S(1)}, s32[]{:T(128)}, /*index=5*/...) while((s32[]{:T(128)}, f32[1,768,1]{1,2,0:T(1,128)S(1)}, ...), condition=%wide.region_7.8_spmd, body=%wide.region_0.7_spmd.sunk | while | flops 369535616 | bytes 12717297 | solution.py:90
  180.4 10.7 %conditional.2 = ((f32[1,768,1]{1,2,0:T(1,128)S(1)}, f32[1,768,1]{1,2,0:T(1,128)S(1)}, f32[1,768,128]{2,1,0:T(8,128)S(1)})) conditional(s32[]{:T(128)} %convert_element_type.73, (f32[1,768,1]{1,2,0:T(1,128)S(1)}, f32[1,768,1]{1,2,0:T(1,128)S(1)}, f32[1,768,128]{2,1,0:T(8,128)S(1)}) %tuple.56, (s32[]{:T(128)}, s32[]{:T(128)}, s32[16]{0:T(128)}, ...), branch_computations={%region_1.0_spmd, %region_2.6_spmd} | conditional | flops 369535616 | bytes 12717050 | solution.py:80
  185.7 3.0 fusion
  189.4 1.8 fusion.5
  191.2 10.7 %conditional.2 = ((f32[1,768,1]{1,2,0:T(1,128)S(1)}, f32[1,768,1]{1,2,0:T(1,128)S(1)}, f32[1,768,128]{2,1,0:T(8,128)S(1)})) conditional(s32[]{:T(128)} %convert_element_type.73, (f32[1,768,1]{1,2,0:T(1,128)S(1)}, f32[1,768,1]{1,2,0:T(1,128)S(1)}, f32[1,768,128]{2,1,0:T(8,128)S(1)}) %tuple.56, (s32[]{:T(128)}, s32[]{:T(128)}, s32[16]{0:T(128)}, ...), branch_computations={%region_1.0_spmd, %region_2.6_spmd} | conditional | flops 369535616 | bytes 12717050 | solution.py:80
  196.5 3.0 fusion
  201.9 10.7 %conditional.2 = ((f32[1,768,1]{1,2,0:T(1,128)S(1)}, f32[1,768,1]{1,2,0:T(1,128)S(1)}, f32[1,768,128]{2,1,0:T(8,128)S(1)})) conditional(s32[]{:T(128)} %convert_element_type.73, (f32[1,768,1]{1,2,0:T(1,128)S(1)}, f32[1,768,1]{1,2,0:T(1,128)S(1)}, f32[1,768,128]{2,1,0:T(8,128)S(1)}) %tuple.56, (s32[]{:T(128)}, s32[]{:T(128)}, s32[16]{0:T(128)}, ...), branch_computations={%region_1.0_spmd, %region_2.6_spmd} | conditional | flops 369535616 | bytes 12717050 | solution.py:80
  207.2 3.0 fusion
  210.9 1.8 fusion.5
  212.7 10.7 %conditional.2 = ((f32[1,768,1]{1,2,0:T(1,128)S(1)}, f32[1,768,1]{1,2,0:T(1,128)S(1)}, f32[1,768,128]{2,1,0:T(8,128)S(1)})) conditional(s32[]{:T(128)} %convert_element_type.73, (f32[1,768,1]{1,2,0:T(1,128)S(1)}, f32[1,768,1]{1,2,0:T(1,128)S(1)}, f32[1,768,128]{2,1,0:T(8,128)S(1)}) %tuple.56, (s32[]{:T(128)}, s32[]{:T(128)}, s32[16]{0:T(128)}, ...), branch_computations={%region_1.0_spmd, %region_2.6_spmd} | conditional | flops 369535616 | bytes 12717050 | solution.py:80
  218.0 3.0 fusion
  223.5 10.7 %conditional.2 = ((f32[1,768,1]{1,2,0:T(1,128)S(1)}, f32[1,768,1]{1,2,0:T(1,128)S(1)}, f32[1,768,128]{2,1,0:T(8,128)S(1)})) conditional(s32[]{:T(128)} %convert_element_type.73, (f32[1,768,1]{1,2,0:T(1,128)S(1)}, f32[1,768,1]{1,2,0:T(1,128)S(1)}, f32[1,768,128]{2,1,0:T(8,128)S(1)}) %tuple.56, (s32[]{:T(128)}, s32[]{:T(128)}, s32[16]{0:T(128)}, ...), branch_computations={%region_1.0_spmd, %region_2.6_spmd} | conditional | flops 369535616 | bytes 12717050 | solution.py:80
  228.8 3.0 fusion
  232.5 1.8 fusion.5
  234.2 10.7 %conditional.2 = ((f32[1,768,1]{1,2,0:T(1,128)S(1)}, f32[1,768,1]{1,2,0:T(1,128)S(1)}, f32[1,768,128]{2,1,0:T(8,128)S(1)})) conditional(s32[]{:T(128)} %convert_element_type.73, (f32[1,768,1]{1,2,0:T(1,128)S(1)}, f32[1,768,1]{1,2,0:T(1,128)S(1)}, f32[1,768,128]{2,1,0:T(8,128)S(1)}) %tuple.56, (s32[]{:T(128)}, s32[]{:T(128)}, s32[16]{0:T(128)}, ...), branch_computations={%region_1.0_spmd, %region_2.6_spmd} | conditional | flops 369535616 | bytes 12717050 | solution.py:80
  239.6 3.0 fusion
  245.0 10.7 %conditional.2 = ((f32[1,768,1]{1,2,0:T(1,128)S(1)}, f32[1,768,1]{1,2,0:T(1,128)S(1)}, f32[1,768,128]{2,1,0:T(8,128)S(1)})) conditional(s32[]{:T(128)} %convert_element_type.73, (f32[1,768,1]{1,2,0:T(1,128)S(1)}, f32[1,768,1]{1,2,0:T(1,128)S(1)}, f32[1,768,128]{2,1,0:T(8,128)S(1)}) %tuple.56, (s32[]{:T(128)}, s32[]{:T(128)}, s32[16]{0:T(128)}, ...), branch_computations={%region_1.0_spmd, %region_2.6_spmd} | conditional | flops 369535616 | bytes 12717050 | solution.py:80
  250.3 3.0 fusion
  254.0 1.8 fusion.5
  255.8 10.7 %conditional.2 = ((f32[1,768,1]{1,2,0:T(1,128)S(1)}, f32[1,768,1]{1,2,0:T(1,128)S(1)}, f32[1,768,128]{2,1,0:T(8,128)S(1)})) conditional(s32[]{:T(128)} %convert_element_type.73, (f32[1,768,1]{1,2,0:T(1,128)S(1)}, f32[1,768,1]{1,2,0:T(1,128)S(1)}, f32[1,768,128]{2,1,0:T(8,128)S(1)}) %tuple.56, (s32[]{:T(128)}, s32[]{:T(128)}, s32[16]{0:T(128)}, ...), branch_computations={%region_1.0_spmd, %region_2.6_spmd} | conditional | flops 369535616 | bytes 12717050 | solution.py:80
  261.1 3.0 fusion
  266.6 10.7 %conditional.2 = ((f32[1,768,1]{1,2,0:T(1,128)S(1)}, f32[1,768,1]{1,2,0:T(1,128)S(1)}, f32[1,768,128]{2,1,0:T(8,128)S(1)})) conditional(s32[]{:T(128)} %convert_element_type.73, (f32[1,768,1]{1,2,0:T(1,128)S(1)}, f32[1,768,1]{1,2,0:T(1,128)S(1)}, f32[1,768,128]{2,1,0:T(8,128)S(1)}) %tuple.56, (s32[]{:T(128)}, s32[]{:T(128)}, s32[16]{0:T(128)}, ...), branch_computations={%region_1.0_spmd, %region_2.6_spmd} | conditional | flops 369535616 | bytes 12717050 | solution.py:80
  271.9 3.0 fusion
  275.5 1.8 fusion.5
  277.3 10.7 %conditional.2 = ((f32[1,768,1]{1,2,0:T(1,128)S(1)}, f32[1,768,1]{1,2,0:T(1,128)S(1)}, f32[1,768,128]{2,1,0:T(8,128)S(1)})) conditional(s32[]{:T(128)} %convert_element_type.73, (f32[1,768,1]{1,2,0:T(1,128)S(1)}, f32[1,768,1]{1,2,0:T(1,128)S(1)}, f32[1,768,128]{2,1,0:T(8,128)S(1)}) %tuple.56, (s32[]{:T(128)}, s32[]{:T(128)}, s32[16]{0:T(128)}, ...), branch_computations={%region_1.0_spmd, %region_2.6_spmd} | conditional | flops 369535616 | bytes 12717050 | solution.py:80
  282.6 3.0 fusion
  288.1 10.7 %conditional.2 = ((f32[1,768,1]{1,2,0:T(1,128)S(1)}, f32[1,768,1]{1,2,0:T(1,128)S(1)}, f32[1,768,128]{2,1,0:T(8,128)S(1)})) conditional(s32[]{:T(128)} %convert_element_type.73, (f32[1,768,1]{1,2,0:T(1,128)S(1)}, f32[1,768,1]{1,2,0:T(1,128)S(1)}, f32[1,768,128]{2,1,0:T(8,128)S(1)}) %tuple.56, (s32[]{:T(128)}, s32[]{:T(128)}, s32[16]{0:T(128)}, ...), branch_computations={%region_1.0_spmd, %region_2.6_spmd} | conditional | flops 369535616 | bytes 12717050 | solution.py:80
  293.4 3.0 fusion
  297.1 1.8 fusion.5
  298.9 10.7 %conditional.2 = ((f32[1,768,1]{1,2,0:T(1,128)S(1)}, f32[1,768,1]{1,2,0:T(1,128)S(1)}, f32[1,768,128]{2,1,0:T(8,128)S(1)})) conditional(s32[]{:T(128)} %convert_element_type.73, (f32[1,768,1]{1,2,0:T(1,128)S(1)}, f32[1,768,1]{1,2,0:T(1,128)S(1)}, f32[1,768,128]{2,1,0:T(8,128)S(1)}) %tuple.56, (s32[]{:T(128)}, s32[]{:T(128)}, s32[16]{0:T(128)}, ...), branch_computations={%region_1.0_spmd, %region_2.6_spmd} | conditional | flops 369535616 | bytes 12717050 | solution.py:80
  304.2 3.0 fusion
  309.6 10.7 %conditional.2 = ((f32[1,768,1]{1,2,0:T(1,128)S(1)}, f32[1,768,1]{1,2,0:T(1,128)S(1)}, f32[1,768,128]{2,1,0:T(8,128)S(1)})) conditional(s32[]{:T(128)} %convert_element_type.73, (f32[1,768,1]{1,2,0:T(1,128)S(1)}, f32[1,768,1]{1,2,0:T(1,128)S(1)}, f32[1,768,128]{2,1,0:T(8,128)S(1)}) %tuple.56, (s32[]{:T(128)}, s32[]{:T(128)}, s32[16]{0:T(128)}, ...), branch_computations={%region_1.0_spmd, %region_2.6_spmd} | conditional | flops 369535616 | bytes 12717050 | solution.py:80
  315.0 3.0 fusion
  318.6 1.8 fusion.5
  320.4 10.7 %conditional.2 = ((f32[1,768,1]{1,2,0:T(1,128)S(1)}, f32[1,768,1]{1,2,0:T(1,128)S(1)}, f32[1,768,128]{2,1,0:T(8,128)S(1)})) conditional(s32[]{:T(128)} %convert_element_type.73, (f32[1,768,1]{1,2,0:T(1,128)S(1)}, f32[1,768,1]{1,2,0:T(1,128)S(1)}, f32[1,768,128]{2,1,0:T(8,128)S(1)}) %tuple.56, (s32[]{:T(128)}, s32[]{:T(128)}, s32[16]{0:T(128)}, ...), branch_computations={%region_1.0_spmd, %region_2.6_spmd} | conditional | flops 369535616 | bytes 12717050 | solution.py:80
  325.7 3.0 fusion
  331.2 10.7 %conditional.2 = ((f32[1,768,1]{1,2,0:T(1,128)S(1)}, f32[1,768,1]{1,2,0:T(1,128)S(1)}, f32[1,768,128]{2,1,0:T(8,128)S(1)})) conditional(s32[]{:T(128)} %convert_element_type.73, (f32[1,768,1]{1,2,0:T(1,128)S(1)}, f32[1,768,1]{1,2,0:T(1,128)S(1)}, f32[1,768,128]{2,1,0:T(8,128)S(1)}) %tuple.56, (s32[]{:T(128)}, s32[]{:T(128)}, s32[16]{0:T(128)}, ...), branch_computations={%region_1.0_spmd, %region_2.6_spmd} | conditional | flops 369535616 | bytes 12717050 | solution.py:80
  336.5 3.0 fusion
  342.0 10.7 %conditional.2 = ((f32[1,768,1]{1,2,0:T(1,128)S(1)}, f32[1,768,1]{1,2,0:T(1,128)S(1)}, f32[1,768,128]{2,1,0:T(8,128)S(1)})) conditional(s32[]{:T(128)} %convert_element_type.73, (f32[1,768,1]{1,2,0:T(1,128)S(1)}, f32[1,768,1]{1,2,0:T(1,128)S(1)}, f32[1,768,128]{2,1,0:T(8,128)S(1)}) %tuple.56, (s32[]{:T(128)}, s32[]{:T(128)}, s32[16]{0:T(128)}, ...), branch_computations={%region_1.0_spmd, %region_2.6_spmd} | conditional | flops 369535616 | bytes 12717050 | solution.py:80
  347.3 3.0 fusion
  353.3 1.8 reduce.16
  355.8 19.1 %all-to-all-start.3 = ((bf16[32,2,1536]{2,1,0:T(2,128)(2,1)}), bf16[32,2,1536]{2,1,0:T(2,128)(2,1)S(1)}, u32[]{:S(2)}, u32[]{:S(2)}) async-start(bf16[32,2,1536]{2,1,0:T(2,128)(2,1)} %reshape.185), calls=%async_computation.3 | async-start | bytes 393216 | tf_op jit(solution)/shard_map/all_to_all | solution.py:142
  376.5 8.0 %all-to-all-done.3 = bf16[32,2,1536]{2,1,0:T(2,128)(2,1)S(1)} async-done(((bf16[32,2,1536]{2,1,0:T(2,128)(2,1)}), bf16[32,2,1536]{2,1,0:T(2,128)(2,1)S(1)}, u32[]{:S(2)}, u32[]{:S(2)}) %all-to-all-start.3) | async-done | bytes 196640 | tf_op jit(solution)/shard_map/all_to_all | solution.py:142
  (236 shorter events, 117.0 us)
Async XLA Ops:
  11.5 34.5 %copy-start.1 = (bf16[1,24,4096]{2,1,0:T(8,128)(2,1)S(1)}, bf16[1,24,4096]{2,1,0:T(8,128)(2,1)}, u32[]{:S(2)}) copy-start(bf16[1,24,4096]{2,1,0:T(8,128)(2,1)} %param.12) | copy-start | bytes 589828
  36.1 37.2 %all-to-all-start.1 = ((bf16[32,2,1536]{2,1,0:T(2,128)(2,1)}), bf16[32,2,1536]{2,1,0:T(2,128)(2,1)S(1)}, u32[]{:S(2)}, u32[]{:S(2)}) async-start(bf16[32,2,1536]{2,1,0:T(2,128)(2,1)} %reshape.179), calls=%async_computation.1 | async-start | bytes 393216 | tf_op jit(solution)/shard_map/all_to_all | solution.py:106
  73.3 19.2 %all-to-all-start = ((bf16[32,2,1536]{2,1,0:T(2,128)(2,1)}), bf16[32,2,1536]{2,1,0:T(2,128)(2,1)S(1)}, u32[]{:S(2)}, u32[]{:S(2)}) async-start(bf16[32,2,1536]{2,1,0:T(2,128)(2,1)} %reshape.181), calls=%async_computation | async-start | bytes 393216 | tf_op jit(solution)/shard_map/all_to_all | solution.py:105
  82.8 97.5 %all-gather.2.cloned.1.call-start = ((), (), s32[]{:S(2)}) async-start(), calls=%async_computation.4 | async-start | bytes 6684672 | tf_op jit(solution)/shard_map/all_gather | solution.py:137
  95.4 3.1 copy-start.2
  125.8 15.1 %all-to-all-start.2 = ((bf16[32,2,1536]{2,1,0:T(2,128)(2,1)}), bf16[32,2,1536]{2,1,0:T(2,128)(2,1)S(1)}, u32[]{:S(2)}, u32[]{:S(2)}) async-start(bf16[32,2,1536]{2,1,0:T(2,128)(2,1)} %reshape.183), calls=%async_computation.2 | async-start | bytes 393216 | tf_op jit(solution)/shard_map/all_to_all | solution.py:104
  352.7 22.2 %copy-start.3 = (s32[16]{0:T(128)S(1)}, s32[16]{0:T(128)}, u32[]{:S(2)}) copy-start(s32[16]{0:T(128)} %param.14) | copy-start | bytes 196
  352.7 23.6 %copy-start = (f32[16,4096]{1,0:T(8,128)S(1)}, f32[16,4096]{1,0:T(8,128)}, u32[]{:S(2)}) copy-start(f32[16,4096]{1,0:T(8,128)} %param.17) | copy-start | bytes 786436
  355.8 28.7 %all-to-all-start.3 = ((bf16[32,2,1536]{2,1,0:T(2,128)(2,1)}), bf16[32,2,1536]{2,1,0:T(2,128)(2,1)S(1)}, u32[]{:S(2)}, u32[]{:S(2)}) async-start(bf16[32,2,1536]{2,1,0:T(2,128)(2,1)} %reshape.185), calls=%async_computation.3 | async-start | bytes 393216 | tf_op jit(solution)/shard_map/all_to_all | solution.py:142
Sparse Core Ops, SparseCore 0:
  98.6 81.6 all-gather.1
where the time goes:
time: 395 us; the launch traced here: 393 us
  other arithmetic  128 us (32%)
  matrix products  115 us (29%)
  waiting for transfers between devices  55.9 us (14%)
  starting transfers between devices  44.3 us (11%)
  local copies, waits for them, and re-layouts  33.5 us (8%)
  between operations  13.7 us (3%)
    unnamed x4, other arithmetic  69.3 us
    dot_general x16, matrix products, update(): jnp.dot(layout_rows, key_sel.T, precision=lax.Precision.HIGHEST) > 0.5  47.4 us
    all_gather x1, waiting for transfers between devices, shards(): lax.all_gather(key_value, 'span', axis=1, tiled=True)  34.2 us
    dot_general x16, matrix products, update(): jnp.einsum('hqk,khd->hqd', exps.astype(jnp.bfloat16), value_part, preferr...  28.2 us
    unnamed x23, local copies, waits for them, and re-layouts  26.5 us
    dot_general x16, matrix products, update(): jnp.einsum('qhd,khd->hqk', query_heads, key_part, preferred_element_type=...  22.3 us
    reduce_sum x16, other arithmetic, update(): own_count = jnp.sum(jnp.where(span_ids == query_span, counts, 0))  21.4 us
    all_to_all x1, starting transfers between devices, shards(): lax.all_to_all(attended[None], 'seq', split_axis=1, concat_axis=2, tiled=...  19.1 us
  transfers between devices with their start and end apart: 5, of which 4 were waited for; matrix products, arithmetic and copies ran while one was open for 17% of the time, Pallas kernels for 0%

commit v1 on v0

v1 whole, which is shorter than its diff:
```python
import functools
import math

import jax
import jax.numpy as jnp
from jax import lax
from jax.experimental import pallas as pl
from jax.experimental.pallas import tpu as pltpu
from jax.sharding import PartitionSpec as P

MESH = pl.DeviceIdType.MESH
HD = 128
FRAMES = 8
SPANS = 16
ROWS = 768
PIECE = 24
PEERS = 32
FRAME_ROWS = ROWS // FRAMES
SCALE = math.log2(math.e) / math.sqrt(HD)
LOW = -1e30
F32, BF16 = jnp.float32, jnp.bfloat16


def whole(ref, sem):
    return pltpu.make_async_copy(ref, ref, sem)


def kernel(
    q_ref, k_ref, v_ref, step_ref, count_ref, layout_ref, gate_ref, out_ref,
    kg, vg, qg, kx, vt, qt, s_buf, m_buf, acc, obuf, part_out, stat_out, part_in, stat_in,
    a2a_send, a2a_recv, ring_send, ring_recv, pair_send, pair_recv,
):
    span = lax.axis_index("span")
    seq = lax.axis_index("seq")
    core = lax.rem(span, 2)
    z_hi = lax.rem(lax.div(span, 2), 2)
    x = lax.div(span, 4)
    z_lo = lax.div(seq, 8)
    y = lax.rem(seq, 8)
    half = lax.rem(z_lo, 2)
    plane = z_hi * 2 + lax.div(z_lo, 2)
    head = plane * 8 + y
    role = (x * 2 + half) * 2 + core
    own = x * 2 + core
    has_self = (half == z_hi).astype(jnp.int32)

    def ring_span(pos):
        return (pos * 2 + z_hi) * 2 + core

    right_x, left_x, far_x = lax.rem(x + 1, 4), lax.rem(x + 3, 4), lax.rem(x + 2, 4)
    right = (ring_span(right_x), seq)
    left = (ring_span(left_x), seq)
    sibling = (span + 1 - 2 * core, seq)
    partner = (span, seq + 8 - 16 * half)

    barrier = pltpu.get_barrier_semaphore()

    def source_of(turn):
        return lax.rem(z_lo + lax.div(turn, 8), 4) * 8 + lax.rem(y + lax.rem(turn, 8), 8)

    def greet(turn, carry):
        pl.semaphore_signal(barrier, inc=1, device_id=(role, source_of(turn)), device_id_type=MESH)
        return carry

    lax.fori_loop(1, PEERS, greet, 0)

    @pl.when(has_self == 0)
    def _():
        greet(0, 0)

    for other in (right, left, sibling, partner):
        pl.semaphore_signal(barrier, inc=1, device_id=other, device_id_type=MESH)
    pl.semaphore_wait(barrier, PEERS + 4 - has_self)

    def scatter(array_ref, landing, which):
        def target(turn):
            to_plane = lax.rem(plane + lax.div(turn, 8), 4)
            to_y = lax.rem(y + lax.rem(turn, 8), 8)
            to_span = (x * 2 + lax.div(to_plane, 2)) * 2 + core
            to_seq = (2 * lax.rem(to_plane, 2) + z_hi) * 8 + to_y
            columns = pl.ds(pl.multiple_of((to_plane * 8 + to_y) * HD, HD), HD)
            return (to_span, to_seq), array_ref.at[:, columns], landing.at[seq]

        def send(turn, carry):
            device, source, destination = target(turn)
            pltpu.make_async_remote_copy(
                src_ref=source, dst_ref=destination, send_sem=a2a_send.at[which],
                recv_sem=a2a_recv.at[which], device_id=device, device_id_type=MESH,
            ).start()
            return carry

        @pl.when(has_self == 1)
        def _():
            _, source, destination = target(0)
            pltpu.make_async_copy(source, destination, a2a_recv.at[which]).start()

        @pl.when(has_self == 0)
        def _():
            send(0, 0)

        lax.fori_loop(1, PEERS, send, 0)

    scatter(k_ref, kg.at[own], 1)
    scatter(q_ref, qg.at[0], 0)
    scatter(v_ref, vg.at[own], 2)

    rows = lax.broadcasted_iota(jnp.int32, (ROWS, HD), 0)
    cols = lax.broadcasted_iota(jnp.int32, (ROWS, HD), 1)
    for item in range(8):
        count = count_ref[(item // 2) * 4 + half * 2 + item % 2]
        hidden = (cols == FRAMES) & (rows >= count * FRAME_ROWS)
        kx[item, :, HD:] = jnp.where(hidden, LOW, 0.0).astype(BF16)
        vt[item, HD:, :] = jnp.ones((16, ROWS), BF16)
    first = cols * FRAME_ROWS
    kx[own, :, HD:] = ((cols < FRAMES) & (rows >= first) & (rows < first + FRAME_ROWS)).astype(F32).astype(BF16)
    frame_id = lax.broadcasted_iota(jnp.int32, (16, ROWS), 0)
    lane = lax.broadcasted_iota(jnp.int32, (16, ROWS), 1)
    own_count = count_ref[role]
    hit = jnp.zeros((16, ROWS), jnp.int32)
    for q_frame in range(FRAMES):
        column = jnp.zeros((16, ROWS), jnp.int32)
        for k_frame in range(FRAMES):
            column = jnp.where(frame_id == k_frame, layout_ref[q_frame, k_frame], column)
        inside = (lane >= q_frame * FRAME_ROWS) & (lane < (q_frame + 1) * FRAME_ROWS)
        hit = jnp.where(inside, column, hit)
    valid = frame_id < own_count
    same = (lane >= frame_id * FRAME_ROWS) & (lane < (frame_id + 1) * FRAME_ROWS)
    shown = (valid & (hit == 1)) | same
    one_row = jnp.where(frame_id == FRAMES, 1.0, 0.0)
    in_frames = frame_id < FRAMES
    qt[0, HD:HD + 16, :] = jnp.where(in_frames & jnp.logical_not(shown), LOW, one_row).astype(BF16)
    qt[1, HD:HD + 16, :] = jnp.where(in_frames & jnp.logical_not(valid), LOW, one_row).astype(BF16)
    qt[:, HD + 16:, :] = jnp.zeros((2, HD - 16, ROWS), BF16)
    m_buf[...] = jnp.full_like(m_buf, LOW)
    acc[...] = jnp.zeros_like(acc)

    gathered = (kg, vg)

    def hop(array, number, item, device, rows_from=0, row_count=PEERS):
        piece = gathered[array].at[item, pl.ds(rows_from, row_count)]
        return pltpu.make_async_remote_copy(
            src_ref=piece, dst_ref=piece, send_sem=ring_send.at[array, number],
            recv_sem=ring_recv.at[array, number], device_id=device, device_id_type=MESH,
        )

    other_core = 1 - core
    left_item, right_item, far_item = left_x * 2 + core, right_x * 2 + core, far_x * 2 + core
    near_half, back_half = PEERS // 2, PEERS // 2

    def outgoing(array):
        return (
            hop(array, 0, own, right),
            hop(array, 1, own, left),
            hop(array, 2, own, sibling),
            hop(array, 3, left_item, right, 0, near_half),
            hop(array, 4, right_item, left, near_half, back_half),
            hop(array, 5, left_item, sibling),
            hop(array, 6, right_item, sibling),
            hop(array, 7, far_item, sibling, 0, near_half),
            hop(array, 8, far_item, sibling, near_half, back_half),
        )

    def incoming(array):
        return (
            hop(array, 0, left_item, right),
            hop(array, 1, right_item, left),
            hop(array, 2, x * 2 + other_core, sibling),
            hop(array, 3, far_item, right, 0, near_half),
            hop(array, 4, far_item, left, near_half, back_half),
            hop(array, 5, left_x * 2 + other_core, sibling),
            hop(array, 6, right_x * 2 + other_core, sibling),
            hop(array, 7, far_x * 2 + other_core, sibling, 0, near_half),
            hop(array, 8, far_x * 2 + other_core, sibling, near_half, back_half),
        )

    k_out, v_out, k_in, v_in = outgoing(0), outgoing(1), incoming(0), incoming(1)

    def flat(piece):
        return piece.astype(F32).reshape(ROWS, HD).astype(BF16)

    def take_keys(item):
        kx[item, :, :HD] = flat(kg[item])

    def take_values(item):
        vt[item, :HD, :] = flat(vg[item]).T

    def scores(slot, item, side):
        result = jnp.dot(kx[item], qt[side], preferred_element_type=F32)
        s_buf[slot] = result
        return jnp.max(result, axis=0, keepdims=True)

    def absorb(slot, item, side, block_max):
        old_max = m_buf[side]
        new_max = jnp.maximum(old_max, block_max)
        weights = jnp.exp2(s_buf[slot] * SCALE - new_max * SCALE).astype(BF16)
        summed = jnp.dot(vt[item], weights, preferred_element_type=F32)
        acc[side] = acc[side] * jnp.exp2((old_max - new_max) * SCALE) + summed
        m_buf[side] = new_max

    def attend(blocks):
        block_max = scores(0, *blocks[0])
        for number, block in enumerate(blocks):
            if number + 1 < len(blocks):
                next_max = scores((number + 1) % 2, *blocks[number + 1])
            absorb(number % 2, *block, block_max)
            if number + 1 < len(blocks):
                block_max = next_max

    def pair(ref_out, ref_in, number):
        return pltpu.make_async_remote_copy(
            src_ref=ref_out, dst_ref=ref_in, send_sem=pair_send.at[number],
            recv_sem=pair_recv.at[number], device_id=partner, device_id_type=MESH,
        )

    swap_queries = pair(qg.at[0], qg.at[1], 0)
    swap_part = pair(part_out, part_in, 1)
    swap_stat = pair(stat_out, stat_in, 2)

    whole(kg.at[own], a2a_recv.at[1]).wait()
    for number in range(3):
        k_out[number].start()
    take_keys(own)
    whole(qg.at[0], a2a_recv.at[0]).wait()
    swap_queries.start()
    qt[0, :HD, :] = flat(qg[0]).T
    whole(vg.at[own], a2a_recv.at[2]).wait()
    for number in range(3):
        v_out[number].start()
    take_values(own)
    attend([(own, 0)])

    for number in (0, 1):
        k_in[number].wait_recv()
    for number in (3, 4, 5, 6):
        k_out[number].start()
    sib = x * 2 + other_core
    k_in[2].wait_recv()
    v_in[2].wait_recv()
    take_keys(sib)
    take_values(sib)
    swap_queries.wait_recv()
    qt[1, :HD, :] = flat(qg[1]).T

    @pl.when(core == 1)
    def _():
        attend([(sib, 0)])

    @pl.when(half == 0)
    def _():
        attend([(own, 1), (sib, 1)])

    for number in (0, 1):
        v_in[number].wait_recv()
    for number in (3, 4, 5, 6):
        v_out[number].start()
    for array in (k_in, v_in):
        for number in (5, 6):
            array[number].wait_recv()

    def column(pos):
        mine, other = pos * 2 + core, pos * 2 + other_core
        for item in (mine, other):
            take_keys(item)
            take_values(item)
        attend([(mine, 1), (other, 1), (mine, 0), (other, 0)])

    @pl.when(x >= 1)
    def _():
        column(left_x)

    for number in (3, 4):
        k_in[number].wait_recv()
    for number in (7, 8):
        k_out[number].start()

    @pl.when(x == 3)
    def _():
        column(right_x)

    for number in (3, 4):
        v_in[number].wait_recv()
    for number in (7, 8):
        v_out[number].start()
    for array in (k_in, v_in):
        for number in (7, 8):
            array[number].wait_recv()

    @pl.when(x >= 2)
    def _():
        column(far_x)

    total = acc[1, HD:HD + 1, :]
    part_out[...] = (acc[1, :HD, :] / jnp.where(total > 0.0, total, 1.0)).astype(BF16)
    stat_out[0:1, :] = m_buf[1]
    stat_out[1:2, :] = total
    stat_out[2:, :] = jnp.zeros((6, ROWS), F32)
    swap_part.start()
    swap_stat.start()
    swap_stat.wait_recv()
    swap_part.wait_recv()
    other_max, other_total = stat_in[0:1, :], stat_in[1:2, :]
    own_max, own_total = m_buf[0], acc[0, HD:HD + 1, :]
    top = jnp.maximum(own_max, other_max)
    own_scale = jnp.exp2((own_max - top) * SCALE)
    other_weight = other_total * jnp.exp2((other_max - top) * SCALE)
    denominator = own_total * own_scale + other_weight
    mixed = (acc[0, :HD, :] * own_scale + part_in[...].astype(F32) * other_weight) / denominator
    gates = gate_ref[:, pl.ds(pl.multiple_of(head * HD, HD), HD)]
    step_id = lax.broadcasted_iota(jnp.int32, gates.shape, 0)
    gate = jnp.sum(jnp.where(step_id == step_ref[role], gates, 0.0), axis=0, keepdims=True)
    attended = mixed.T.astype(BF16).astype(F32) * gate
    obuf[...] = attended.reshape(PEERS, PIECE, HD).astype(BF16)

    columns = pl.ds(pl.multiple_of(head * HD, HD), HD)

    def give(turn, carry):
        to_seq = source_of(turn)
        pltpu.make_async_remote_copy(
            src_ref=obuf.at[to_seq], dst_ref=out_ref.at[:, columns], send_sem=a2a_send.at[3],
            recv_sem=a2a_recv.at[3], device_id=(role, to_seq), device_id_type=MESH,
        ).start()
        return carry

    @pl.when(has_self == 1)
    def _():
        pltpu.make_async_copy(obuf.at[seq], out_ref.at[:, columns], a2a_recv.at[3]).start()

    @pl.when(has_self == 0)
    def _():
        give(0, 0)

    lax.fori_loop(1, PEERS, give, 0)

    for array in (k_out, v_out):
        for copy in array:
            copy.wait_send()
    for copy in (swap_queries, swap_part, swap_stat):
        copy.wait_send()
    whole(out_ref, a2a_recv.at[3]).wait()

    @pl.when(has_self == 1)
    def _():
        for which in range(4):
            whole(obuf.at[pl.ds(0, PEERS - 1)], a2a_send.at[which]).wait()

    @pl.when(has_self == 0)
    def _():
        for which in range(4):
            whole(obuf, a2a_send.at[which]).wait()


def shards(queries, keys, values, step_index, frame_counts, frame_layout, gate_table):
    vmem = pl.BlockSpec(memory_space=pltpu.VMEM)
    smem = pl.BlockSpec(memory_space=pltpu.SMEM)
    piece = (PEERS, PIECE, HD)
    result = pl.pallas_call(
        kernel,
        out_shape=jax.ShapeDtypeStruct(queries.shape[1:], BF16),
        in_specs=[vmem, vmem, vmem, smem, smem, smem, vmem],
        out_specs=vmem,
        scratch_shapes=[
            pltpu.VMEM((8, *piece), BF16),
            pltpu.VMEM((8, *piece), BF16),
            pltpu.VMEM((2, *piece), BF16),
            pltpu.VMEM((8, ROWS, 2 * HD), BF16),
            pltpu.VMEM((8, HD + 16, ROWS), BF16),
            pltpu.VMEM((2, 2 * HD, ROWS), BF16),
            pltpu.VMEM((2, ROWS, ROWS), F32),
            pltpu.VMEM((2, 1, ROWS), F32),
            pltpu.VMEM((2, HD + 16, ROWS), F32),
            pltpu.VMEM(piece, BF16),
            pltpu.VMEM((HD, ROWS), BF16),
            pltpu.VMEM((8, ROWS), F32),
            pltpu.VMEM((HD, ROWS), BF16),
            pltpu.VMEM((8, ROWS), F32),
            pltpu.SemaphoreType.DMA((4,)),
            pltpu.SemaphoreType.DMA((4,)),
            pltpu.SemaphoreType.DMA((2, 9)),
            pltpu.SemaphoreType.DMA((2, 9)),
            pltpu.SemaphoreType.DMA((3,)),
            pltpu.SemaphoreType.DMA((3,)),
        ],
        compiler_params=pltpu.CompilerParams(
            collective_id=0, has_side_effects=True, vmem_limit_bytes=48 << 20
        ),
    )(queries[0], keys[0], values[0], step_index, frame_counts, frame_layout, gate_table)
    return result[None]


def solution(mesh):
    split = P("span", "seq", None)
    return jax.shard_map(
        shards,
        mesh=mesh,
        in_specs=(split, split, split, P(), P(), P(), P()),
        out_specs=split,
        check_vma=False,
    )
```

time: 395 us -> 78.4 us (0.20)
  the two profiles are of different devices: /device:TPU:271 before, /device:TPU:6 now
where the time goes in v1:
time: 78.4 us; the launch traced here: 78.2 us
  Pallas kernels  73.1 us (93%)
  local copies, waits for them, and re-layouts  5.1 us (7%)
    pallas_call x1, Pallas kernels, shards(): pl.pallas_call(kernel, out_shape=jax.ShapeDtypeStruct(queries.shape[1:],...  73.1 us
    unnamed x15, local copies, waits for them, and re-layouts  5.1 us

profile of v1, /device:TPU:6, one launch (start us, length us, event | category | flops | bytes accessed | tf_op | source)
XLA Modules:
  0.0 78.2 jit_solution(8921574480204432788)
XLA Ops:
  0.0 0.0 copy-start.4
  0.0 0.0 copy-start.5
  0.0 0.0 copy-start.6
  0.0 0.7 copy-done.4
  0.7 0.0 copy-done.5
  0.7 0.0 copy-done.6
  0.7 0.0 copy-start
  0.7 0.9 %copy-done = f32[16,4096]{1,0:T(8,128)S(1)} copy-done((f32[16,4096]{1,0:T(8,128)S(1)}, f32[16,4096]{1,0:T(8,128)}, u32[]{:S(2)}) %copy-start) | copy-done | bytes 262168
  1.6 0.0 copy-start.1
  1.6 0.9 %copy-done.1 = bf16[1,24,4096]{2,1,0:T(8,128)(2,1)S(1)} copy-done((bf16[1,24,4096]{2,1,0:T(8,128)(2,1)S(1)}, bf16[1,24,4096]{2,1,0:T(8,128)(2,1)}, u32[]{:S(2)}) %copy-start.1) | copy-done | bytes 196632
  2.6 0.0 copy-start.2
  2.6 0.9 %copy-done.2 = bf16[1,24,4096]{2,1,0:T(8,128)(2,1)S(1)} copy-done((bf16[1,24,4096]{2,1,0:T(8,128)(2,1)S(1)}, bf16[1,24,4096]{2,1,0:T(8,128)(2,1)}, u32[]{:S(2)}) %copy-start.2) | copy-done | bytes 196632
  3.5 0.0 copy-start.3
  3.5 0.9 %copy-done.3 = bf16[1,24,4096]{2,1,0:T(8,128)(2,1)S(1)} copy-done((bf16[1,24,4096]{2,1,0:T(8,128)(2,1)S(1)}, bf16[1,24,4096]{2,1,0:T(8,128)(2,1)}, u32[]{:S(2)}) %copy-start.3) | copy-done | bytes 196632
  4.4 73.1 %shard_map.73 = bf16[24,4096]{1,0:T(8,128)(2,1)S(1)} custom-call(bf16[24,4096]{1,0:T(8,128)(2,1)S(1)} %bitcast.5, bf16[24,4096]{1,0:T(8,128)(2,1)S(1)} %bitcast.6, bf16[24,4096]{1,0:T(8,128)(2,1)S(1)} %bitcast.7, s32[16]{0:T(128)S(1)} %copy-done.5, s32[16]{0:T(128)S(1)} %copy-done.6, s32[8,8]{1,0:T(8,128)S(1)} %copy-done.4, f32[16,4096]{1,0:T(8,128)S(1)} %copy-done), custom_call_target="tpu_custom_call" | custom-call | tf_op jit(solution)/shard_map/pallas_call | solution.py:356
  77.5 0.7 copy.9
Async XLA Ops:
  0.0 0.7 copy-start.4
  0.0 0.7 copy-start.5
  0.0 0.7 copy-start.6
  0.7 1.0 %copy-start = (f32[16,4096]{1,0:T(8,128)S(1)}, f32[16,4096]{1,0:T(8,128)}, u32[]{:S(2)}) copy-start(f32[16,4096]{1,0:T(8,128)} %gate_ref.1) | copy-start | bytes 786436
  1.6 0.9 %copy-start.1 = (bf16[1,24,4096]{2,1,0:T(8,128)(2,1)S(1)}, bf16[1,24,4096]{2,1,0:T(8,128)(2,1)}, u32[]{:S(2)}) copy-start(bf16[1,24,4096]{2,1,0:T(8,128)(2,1)} %param.7) | copy-start | bytes 589828
  2.6 0.9 %copy-start.2 = (bf16[1,24,4096]{2,1,0:T(8,128)(2,1)S(1)}, bf16[1,24,4096]{2,1,0:T(8,128)(2,1)}, u32[]{:S(2)}) copy-start(bf16[1,24,4096]{2,1,0:T(8,128)(2,1)} %param.8) | copy-start | bytes 589828
  3.5 0.9 %copy-start.3 = (bf16[1,24,4096]{2,1,0:T(8,128)(2,1)S(1)}, bf16[1,24,4096]{2,1,0:T(8,128)(2,1)}, u32[]{:S(2)}) copy-start(bf16[1,24,4096]{2,1,0:T(8,128)(2,1)} %param.9) | copy-start | bytes 589828

commit v2 on v1

--- a/solution.py
+++ b/solution.py
@@ -21,13 +21,17 @@
 F32, BF16 = jnp.float32, jnp.bfloat16
 
 
+def flip(plane):
+    return 1 - lax.rem(lax.div(plane + 1, 2), 2)
+
+
 def whole(ref, sem):
     return pltpu.make_async_copy(ref, ref, sem)
 
 
 def kernel(
-    q_ref, k_ref, v_ref, step_ref, count_ref, layout_ref, gate_ref, out_ref,
-    kg, vg, qg, kx, vt, qt, s_buf, m_buf, acc, obuf, part_out, stat_out, part_in, stat_in,
+    q_hbm, k_hbm, v_hbm, step_hbm, count_hbm, layout_hbm, gate_hbm, out_ref,
+    q_ref, k_ref, v_ref, step_ref, count_ref, layout_ref, gate_ref, load_sem, kg, vg, qg, kx, vt, qt, s_buf, m_buf, acc, obuf, part_out, stat_out, part_in, stat_in,
     a2a_send, a2a_recv, ring_send, ring_recv, pair_send, pair_recv,
 ):
     span = lax.axis_index("span")
@@ -37,8 +41,9 @@
     x = lax.div(span, 4)
     z_lo = lax.div(seq, 8)
     y = lax.rem(seq, 8)
-    half = lax.rem(z_lo, 2)
+    bit = lax.rem(z_lo, 2)
     plane = z_hi * 2 + lax.div(z_lo, 2)
+    half = lax.rem(bit + flip(plane), 2)
     head = plane * 8 + y
     role = (x * 2 + half) * 2 + core
     own = x * 2 + core
@@ -51,7 +56,18 @@
     right = (ring_span(right_x), seq)
     left = (ring_span(left_x), seq)
     sibling = (span + 1 - 2 * core, seq)
-    partner = (span, seq + 8 - 16 * half)
+    partner = (span, seq + 8 - 16 * bit)
+
+    columns = pl.ds(pl.multiple_of(head * HD, HD), HD)
+    loads = [
+        pltpu.make_async_copy(source, target, load_sem.at[number])
+        for number, (source, target) in enumerate((
+            (k_hbm, k_ref), (v_hbm, v_ref), (q_hbm, q_ref), (count_hbm, count_ref), (layout_hbm, layout_ref),
+            (step_hbm, step_ref), (gate_hbm.at[:, columns], gate_ref),
+        ))
+    ]
+    for load in loads:
+        load.start()
 
     barrier = pltpu.get_barrier_semaphore()
 
@@ -70,14 +86,16 @@
 
     for other in (right, left, sibling, partner):
         pl.semaphore_signal(barrier, inc=1, device_id=other, device_id_type=MESH)
-    pl.semaphore_wait(barrier, PEERS + 4 - has_self)
+    for load in loads:
+        load.wait()
 
     def scatter(array_ref, landing, which):
         def target(turn):
             to_plane = lax.rem(plane + lax.div(turn, 8), 4)
             to_y = lax.rem(y + lax.rem(turn, 8), 8)
             to_span = (x * 2 + lax.div(to_plane, 2)) * 2 + core
-            to_seq = (2 * lax.rem(to_plane, 2) + z_hi) * 8 + to_y
+            to_bit = lax.rem(flip(to_plane) + z_hi, 2)
+            to_seq = (2 * lax.rem(to_plane, 2) + to_bit) * 8 + to_y
             columns = pl.ds(pl.multiple_of((to_plane * 8 + to_y) * HD, HD), HD)
             return (to_span, to_seq), array_ref.at[:, columns], landing.at[seq]
 
@@ -99,10 +117,6 @@
             send(0, 0)
 
         lax.fori_loop(1, PEERS, send, 0)
-
-    scatter(k_ref, kg.at[own], 1)
-    scatter(q_ref, qg.at[0], 0)
-    scatter(v_ref, vg.at[own], 2)
 
     rows = lax.broadcasted_iota(jnp.int32, (ROWS, HD), 0)
     cols = lax.broadcasted_iota(jnp.int32, (ROWS, HD), 1)
@@ -134,6 +148,10 @@
     m_buf[...] = jnp.full_like(m_buf, LOW)
     acc[...] = jnp.zeros_like(acc)
 
+    pl.semaphore_wait(barrier, PEERS + 4 - has_self)
+    scatter(k_ref, kg.at[own], 1)
+    scatter(v_ref, vg.at[own], 2)
+
     gathered = (kg, vg)
 
     def hop(array, number, item, device, rows_from=0, row_count=PEERS):
@@ -145,32 +163,36 @@
 
     other_core = 1 - core
     left_item, right_item, far_item = left_x * 2 + core, right_x * 2 + core, far_x * 2 + core
-    near_half, back_half = PEERS // 2, PEERS // 2
+    lower, upper = (0, PEERS // 2), (PEERS // 2, PEERS // 2)
 
     def outgoing(array):
         return (
-            hop(array, 0, own, right),
-            hop(array, 1, own, left),
-            hop(array, 2, own, sibling),
-            hop(array, 3, left_item, right, 0, near_half),
-            hop(array, 4, right_item, left, near_half, back_half),
-            hop(array, 5, left_item, sibling),
-            hop(array, 6, right_item, sibling),
-            hop(array, 7, far_item, sibling, 0, near_half),
-            hop(array, 8, far_item, sibling, near_half, back_half),
+            hop(array, 0, own, right, *lower),
+            hop(array, 1, own, right, *upper),
+            hop(array, 2, own, left, *upper),
+            hop(array, 3, own, left, *lower),
+            hop(array, 4, own, sibling),
+            hop(array, 5, left_item, right, *lower),
+            hop(array, 6, right_item, left, *upper),
+            hop(array, 7, left_item, sibling),
+            hop(array, 8, right_item, sibling),
+            hop(array, 9, far_item, sibling, *lower),
+            hop(array, 10, far_item, sibling, *upper),
         )
 
     def incoming(array):
         return (
-            hop(array, 0, left_item, right),
-            hop(array, 1, right_item, left),
-            hop(array, 2, x * 2 + other_core, sibling),
-            hop(array, 3, far_item, right, 0, near_half),
-            hop(array, 4, far_item, left, near_half, back_half),
-            hop(array, 5, left_x * 2 + other_core, sibling),
-            hop(array, 6, right_x * 2 + other_core, sibling),
-            hop(array, 7, far_x * 2 + other_core, sibling, 0, near_half),
-            hop(array, 8, far_x * 2 + other_core, sibling, near_half, back_half),
+            hop(array, 0, left_item, right, *lower),
+            hop(array, 1, left_item, right, *upper),
+            hop(array, 2, right_item, left, *upper),
+            hop(array, 3, right_item, left, *lower),
+            hop(array, 4, x * 2 + other_core, sibling),
+            hop(array, 5, far_item, right, *lower),
+            hop(array, 6, far_item, left, *upper),
+            hop(array, 7, left_x * 2 + other_core, sibling),
+            hop(array, 8, right_x * 2 + other_core, sibling),
+            hop(array, 9, far_x * 2 + other_core, sibling, *lower),
+            hop(array, 10, far_x * 2 + other_core, sibling, *upper),
         )
 
     k_out, v_out, k_in, v_in = outgoing(0), outgoing(1), incoming(0), incoming(1)
@@ -216,78 +238,99 @@
     swap_part = pair(part_out, part_in, 1)
     swap_stat = pair(stat_out, stat_in, 2)
 
+    sib = x * 2 + other_core
+
+    def begin(copies):
+        for number in (0, 2, 1, 3, 4):
+            copies[number].start()
+
+    def relay(arriving, leaving):
+        arriving[0].wait_recv()
+        leaving[5].start()
+        arriving[2].wait_recv()
+        leaving[6].start()
+        arriving[1].wait_recv()
+        leaving[7].start()
+        arriving[3].wait_recv()
+        leaving[8].start()
+
+    def finish(arriving, leaving):
+        for number in (5, 6):
+            arriving[number].wait_recv()
+            leaving[number + 4].start()
+
     whole(kg.at[own], a2a_recv.at[1]).wait()
-    for number in range(3):
-        k_out[number].start()
+    begin(k_out)
+    scatter(q_ref, qg.at[0], 0)
     take_keys(own)
+    whole(vg.at[own], a2a_recv.at[2]).wait()
+    begin(v_out)
+    take_values(own)
+    relay(k_in, k_out)
     whole(qg.at[0], a2a_recv.at[0]).wait()
     swap_queries.start()
     qt[0, :HD, :] = flat(qg[0]).T
-    whole(vg.at[own], a2a_recv.at[2]).wait()
-    for number in range(3):
-        v_out[number].start()
-    take_values(own)
+    relay(v_in, v_out)
+    finish(k_in, k_out)
     attend([(own, 0)])
-
-    for number in (0, 1):
-        k_in[number].wait_recv()
-    for number in (3, 4, 5, 6):
-        k_out[number].start()
-    sib = x * 2 + other_core
-    k_in[2].wait_recv()
-    v_in[2].wait_recv()
+    k_in[4].wait_recv()
+    v_in[4].wait_recv()
     take_keys(sib)
     take_values(sib)
-    swap_queries.wait_recv()
-    qt[1, :HD, :] = flat(qg[1]).T
 
     @pl.when(core == 1)
     def _():
         attend([(sib, 0)])
 
-    @pl.when(half == 0)
-    def _():
-        attend([(own, 1), (sib, 1)])
-
-    for number in (0, 1):
-        v_in[number].wait_recv()
-    for number in (3, 4, 5, 6):
-        v_out[number].start()
-    for array in (k_in, v_in):
-        for number in (5, 6):
-            array[number].wait_recv()
-
-    def column(pos):
-        mine, other = pos * 2 + core, pos * 2 + other_core
-        for item in (mine, other):
-            take_keys(item)
-            take_values(item)
-        attend([(mine, 1), (other, 1), (mine, 0), (other, 0)])
-
-    @pl.when(x >= 1)
-    def _():
-        column(left_x)
-
-    for number in (3, 4):
-        k_in[number].wait_recv()
-    for number in (7, 8):
-        k_out[number].start()
-
-    @pl.when(x == 3)
-    def _():
-        column(right_x)
-
-    for number in (3, 4):
-        v_in[number].wait_recv()
-    for number in (7, 8):
-        v_out[number].start()
     for array in (k_in, v_in):
         for number in (7, 8):
             array[number].wait_recv()
 
+    def pair_of(pos):
+        return pos * 2 + core, pos * 2 + other_core
+
+    def take(pos):
+        for item in pair_of(pos):
+            take_keys(item)
+            take_values(item)
+
+    def both(pos, side):
+        return [(item, side) for item in pair_of(pos)]
+
+    @pl.when(x >= 1)
+    def _():
+        take(left_x)
+        attend(both(left_x, 0))
+
+    finish(v_in, v_out)
+
+    @pl.when(x == 3)
+    def _():
+        take(right_x)
+
+    swap_queries.wait_recv()
+    qt[1, :HD, :] = flat(qg[1]).T
+
+    @pl.when(half == 0)
+    def _():
+        attend(both(x, 1))
+
+    @pl.when((x == 1) | (x == 2))
+    def _():
+        attend(both(left_x, 1))
+
+    @pl.when(x == 3)
+    def _():
+        attend(both(left_x, 1) + both(right_x, 1))
+
+    for array in (k_in, v_in):
+        for number in (9, 10):
+            array[number].wait_recv()
+
     @pl.when(x >= 2)
     def _():
-        column(far_x)
+        take(far_x)
+        attend(both(far_x, 1))
 
     total = acc[1, HD:HD + 1, :]
     part_out[...] = (acc[1, :HD, :] / jnp.where(total > 0.0, total, 1.0)).astype(BF16)
@@ -296,6 +339,15 @@
     stat_out[2:, :] = jnp.zeros((6, ROWS), F32)
     swap_part.start()
     swap_stat.start()
+
+    @pl.when(x == 3)
+    def _():
+        attend(both(right_x, 0) + both(far_x, 0))
+
+    @pl.when(x == 2)
+    def _():
+        attend(both(far_x, 0))
+
     swap_stat.wait_recv()
     swap_part.wait_recv()
     other_max, other_total = stat_in[0:1, :], stat_in[1:2, :]
@@ -305,13 +357,11 @@
     other_weight = other_total * jnp.exp2((other_max - top) * SCALE)
     denominator = own_total * own_scale + other_weight
     mixed = (acc[0, :HD, :] * own_scale + part_in[...].astype(F32) * other_weight) / denominator
-    gates = gate_ref[:, pl.ds(pl.multiple_of(head * HD, HD), HD)]
+    gates = gate_ref[...]
     step_id = lax.broadcasted_iota(jnp.int32, gates.shape, 0)
     gate = jnp.sum(jnp.where(step_id == step_ref[role], gates, 0.0), axis=0, keepdims=True)
     attended = mixed.T.astype(BF16).astype(F32) * gate
     obuf[...] = attended.reshape(PEERS, PIECE, HD).astype(BF16)
-
-    columns = pl.ds(pl.multiple_of(head * HD, HD), HD)
 
     def give(turn, carry):
         to_seq = source_of(turn)
@@ -350,15 +400,23 @@
 
 
 def shards(queries, keys, values, step_index, frame_counts, frame_layout, gate_table):
-    vmem = pl.BlockSpec(memory_space=pltpu.VMEM)
-    smem = pl.BlockSpec(memory_space=pltpu.SMEM)
+    anywhere = pl.BlockSpec(memory_space=pl.ANY)
+    block = queries.shape[1:]
     piece = (PEERS, PIECE, HD)
     result = pl.pallas_call(
         kernel,
-        out_shape=jax.ShapeDtypeStruct(queries.shape[1:], BF16),
-        in_specs=[vmem, vmem, vmem, smem, smem, smem, vmem],
-        out_specs=vmem,
+        out_shape=jax.ShapeDtypeStruct(block, BF16),
+        in_specs=[anywhere] * 7,
+        out_specs=pl.BlockSpec(memory_space=pltpu.VMEM),
         scratch_shapes=[
+            pltpu.VMEM(block, BF16),
+            pltpu.VMEM(block, BF16),
+            pltpu.VMEM(block, BF16),
+            pltpu.SMEM(step_index.shape, jnp.int32),
+            pltpu.SMEM(frame_counts.shape, jnp.int32),
+            pltpu.SMEM(frame_layout.shape, jnp.int32),
+            pltpu.VMEM((gate_table.shape[0], HD), F32),
+            pltpu.SemaphoreType.DMA((7,)),
             pltpu.VMEM((8, *piece), BF16),
             pltpu.VMEM((8, *piece), BF16),
             pltpu.VMEM((2, *piece), BF16),
@@ -375,13 +433,13 @@
             pltpu.VMEM((8, ROWS), F32),
             pltpu.SemaphoreType.DMA((4,)),
             pltpu.SemaphoreType.DMA((4,)),
-            pltpu.SemaphoreType.DMA((2, 9)),
-            pltpu.SemaphoreType.DMA((2, 9)),
+            pltpu.SemaphoreType.DMA((2, 11)),
+            pltpu.SemaphoreType.DMA((2, 11)),
             pltpu.SemaphoreType.DMA((3,)),
             pltpu.SemaphoreType.DMA((3,)),
         ],
         compiler_params=pltpu.CompilerParams(
-            collective_id=0, has_side_effects=True, vmem_limit_bytes=48 << 20
+            collective_id=0, has_side_effects=True, vmem_limit_bytes=60 << 20
         ),
     )(queries[0], keys[0], values[0], step_index, frame_counts, frame_layout, gate_table)
     return result[None]

time: 78.4 us -> 61.5 us (0.78)
  Pallas kernels: 73.1 us -> 59.7 us
  local copies, waits for them, and re-layouts: 5.1 us -> 1.62 us
    pallas_call x1, Pallas kernels: 73.1 us -> 59.7 us  [shards(): pl.pallas_call(kernel, out_shape=jax.ShapeDtypeStruct(block, BF16), in_sp...]
    unnamed x15 -> x1, local copies, waits for them, and re-layouts: 5.1 us -> 1.62 us
where the time goes in v2:
time: 61.5 us; the launch traced here: 61.4 us
  Pallas kernels  59.7 us (97%)
  local copies, waits for them, and re-layouts  1.62 us (3%)
    pallas_call x1, Pallas kernels, shards(): pl.pallas_call(kernel, out_shape=jax.ShapeDtypeStruct(block, BF16), in_sp...  59.7 us
    unnamed x1, local copies, waits for them, and re-layouts  1.62 us

profile of v2, /device:TPU:6, one launch (start us, length us, event | category | flops | bytes accessed | tf_op | source)
XLA Modules:
  0.0 61.4 jit_solution(7883042024308874573)
XLA Ops:
  0.0 59.7 %shard_map.73 = bf16[24,4096]{1,0:T(8,128)(2,1)} custom-call(bf16[24,4096]{1,0:T(8,128)(2,1)} %bitcast.5, bf16[24,4096]{1,0:T(8,128)(2,1)} %bitcast.6, bf16[24,4096]{1,0:T(8,128)(2,1)} %bitcast.7, s32[16]{0:T(128)} %step_hbm.1, s32[16]{0:T(128)} %count_hbm.1, s32[8,8]{1,0:T(8,128)} %layout_hbm.1, f32[16,4096]{1,0:T(8,128)} %gate_hbm.1), custom_call_target="tpu_custom_call" | custom-call | tf_op jit(solution)/shard_map/pallas_call | solution.py:406
  59.7 1.6 %copy.9 = bf16[1,24,4096]{2,1,0:T(8,128)(2,1)} copy(bf16[1,24,4096]{2,1,0:T(8,128)(2,1)} %bitcast.4) | data formatting | bytes 393216

commit v3 on v2

--- a/solution.py
+++ b/solution.py
@@ -103,20 +103,29 @@
             device, source, destination = target(turn)
             pltpu.make_async_remote_copy(
                 src_ref=source, dst_ref=destination, send_sem=a2a_send.at[which],
-                recv_sem=a2a_recv.at[which], device_id=device, device_id_type=MESH,
+                recv_sem=a2a_recv.at[which, lax.div(z_lo, 2)], device_id=device, device_id_type=MESH,
             ).start()
             return carry
 
         @pl.when(has_self == 1)
         def _():
             _, source, destination = target(0)
-            pltpu.make_async_copy(source, destination, a2a_recv.at[which]).start()
+            pltpu.make_async_copy(source, destination, a2a_recv.at[which, lax.div(z_lo, 2)]).start()
 
         @pl.when(has_self == 0)
         def _():
             send(0, 0)
 
         lax.fori_loop(1, PEERS, send, 0)
+
+    def sent(which):
+        @pl.when(has_self == 1)
+        def _():
+            whole(obuf.at[pl.ds(0, PEERS - 1)], a2a_send.at[which]).wait()
+
+        @pl.when(has_self == 0)
+        def _():
+            whole(obuf, a2a_send.at[which]).wait()
 
     rows = lax.broadcasted_iota(jnp.int32, (ROWS, HD), 0)
     cols = lax.broadcasted_iota(jnp.int32, (ROWS, HD), 1)
@@ -149,8 +158,6 @@
     acc[...] = jnp.zeros_like(acc)
 
     pl.semaphore_wait(barrier, PEERS + 4 - has_self)
-    scatter(k_ref, kg.at[own], 1)
-    scatter(v_ref, vg.at[own], 2)
 
     gathered = (kg, vg)
 
@@ -163,7 +170,12 @@
 
     other_core = 1 - core
     left_item, right_item, far_item = left_x * 2 + core, right_x * 2 + core, far_x * 2 + core
-    lower, upper = (0, PEERS // 2), (PEERS // 2, PEERS // 2)
+    late = (plane == 2 * half).astype(jnp.int32)
+    early = 1 - late
+    lower, upper = (early * (PEERS // 2), PEERS // 2), (late * (PEERS // 2), PEERS // 2)
+
+    def arrived(array_ref, which, part):
+        whole(array_ref.at[pl.ds(part * (PEERS // 2), PEERS // 2)], a2a_recv.at[which, part]).wait()
 
     def outgoing(array):
         return (
@@ -234,41 +246,88 @@
             recv_sem=pair_recv.at[number], device_id=partner, device_id_type=MESH,
         )
 
-    swap_queries = pair(qg.at[0], qg.at[1], 0)
-    swap_part = pair(part_out, part_in, 1)
-    swap_stat = pair(stat_out, stat_in, 2)
+    swap_early = pair(qg.at[0, pl.ds(*lower)], qg.at[1, pl.ds(*lower)], 0)
+    swap_late = pair(qg.at[0, pl.ds(*upper)], qg.at[1, pl.ds(*upper)], 1)
+    half_rows = (pl.ds(0, ROWS // 2), pl.ds(ROWS // 2, ROWS // 2))
+    swap_parts = [pair(part_out.at[:, at], part_in.at[:, at], 2 + number) for number, at in enumerate(half_rows)]
+    swap_stat = pair(stat_out, stat_in, 4)
 
     sib = x * 2 + other_core
 
-    def begin(copies):
-        for number in (0, 2, 1, 3, 4):
-            copies[number].start()
+    last = x == 3
+    sends_own, has_left_item, has_right_item, has_far_item = x != 3, x != 0, x != 2, x != 1
+    always = x >= 0
+    needed = (sends_own,) * 4 + (always, has_left_item, has_right_item, has_left_item, has_right_item, has_far_item, has_far_item)
+    expected = (has_left_item,) * 2 + (has_right_item,) * 2 + (always, has_far_item, has_far_item) + needed[7:]
+
+    def start(copies, *numbers):
+        for number in numbers:
+            pl.when(needed[number])(copies[number].start)
+
+    def wait(copies, *numbers):
+        for number in numbers:
+            pl.when(expected[number])(copies[number].wait_recv)
+
+    def begin(array, which, copies):
+        arrived(array.at[own], which, early)
+        start(copies, 0, 3)
+        arrived(array.at[own], which, late)
+        start(copies, 2, 1, 4)
 
     def relay(arriving, leaving):
-        arriving[0].wait_recv()
-        leaving[5].start()
-        arriving[2].wait_recv()
-        leaving[6].start()
-        arriving[1].wait_recv()
-        leaving[7].start()
-        arriving[3].wait_recv()
-        leaving[8].start()
+        wait(arriving, 0)
+        start(leaving, 5)
+        wait(arriving, 3, 2)
+        start(leaving, 6, 8)
+        wait(arriving, 1)
+        start(leaving, 7)
 
     def finish(arriving, leaving):
         for number in (5, 6):
-            arriving[number].wait_recv()
-            leaving[number + 4].start()
-
-    whole(kg.at[own], a2a_recv.at[1]).wait()
-    begin(k_out)
-    scatter(q_ref, qg.at[0], 0)
+            wait(arriving, number)
+            start(leaving, number + 4)
+
+    def exchange_queries():
+        for part, swap in ((early, swap_early), (late, swap_late)):
+            arrived(qg.at[0], 0, part)
+            swap.start()
+
+    @pl.when(last)
+    def _():
+        scatter(q_ref, qg.at[0], 0)
+        sent(0)
+        scatter(k_ref, kg.at[own], 1)
+        exchange_queries()
+        sent(1)
+        scatter(v_ref, vg.at[own], 2)
+
+    @pl.when(sends_own)
+    def _():
+        scatter(k_ref, kg.at[own], 1)
+        sent(1)
+        scatter(v_ref, vg.at[own], 2)
+
+    begin(kg, 1, k_out)
+
+    @pl.when(sends_own)
+    def _():
+        sent(2)
+        scatter(q_ref, qg.at[0], 0)
+
     take_keys(own)
-    whole(vg.at[own], a2a_recv.at[2]).wait()
-    begin(v_out)
+
+    @pl.when(last)
+    def _():
+        relay(k_in, k_out)
+
+    begin(vg, 2, v_out)
     take_values(own)
-    relay(k_in, k_out)
-    whole(qg.at[0], a2a_recv.at[0]).wait()
-    swap_queries.start()
+
+    @pl.when(sends_own)
+    def _():
+        relay(k_in, k_out)
+        exchange_queries()
+
     qt[0, :HD, :] = flat(qg[0]).T
     relay(v_in, v_out)
     finish(k_in, k_out)
@@ -283,8 +342,7 @@
         attend([(sib, 0)])
 
     for array in (k_in, v_in):
-        for number in (7, 8):
-            array[number].wait_recv()
+        wait(array, 7, 8)
 
     def pair_of(pos):
         return pos * 2 + core, pos * 2 + other_core
@@ -294,109 +352,107 @@
             take_keys(item)
             take_values(item)
 
-    def both(pos, side):
-        return [(item, side) for item in pair_of(pos)]
-
     @pl.when(x >= 1)
     def _():
         take(left_x)
-        attend(both(left_x, 0))
-
-    finish(v_in, v_out)
-
-    @pl.when(x == 3)
-    def _():
-        take(right_x)
-
-    swap_queries.wait_recv()
-    qt[1, :HD, :] = flat(qg[1]).T
-
-    @pl.when(half == 0)
-    def _():
-        attend(both(x, 1))
-
-    @pl.when((x == 1) | (x == 2))
-    def _():
-        attend(both(left_x, 1))
-
-    @pl.when(x == 3)
-    def _():
-        attend(both(left_x, 1) + both(right_x, 1))
-
-    for array in (k_in, v_in):
-        for number in (9, 10):
-            array[number].wait_recv()
-
-    @pl.when(x >= 2)
-    def _():
-        take(far_x)
-        attend(both(far_x, 1))
-
-    total = acc[1, HD:HD + 1, :]
-    part_out[...] = (acc[1, :HD, :] / jnp.where(total > 0.0, total, 1.0)).astype(BF16)
-    stat_out[0:1, :] = m_buf[1]
-    stat_out[1:2, :] = total
-    stat_out[2:, :] = jnp.zeros((6, ROWS), F32)
-    swap_part.start()
-    swap_stat.start()
-
-    @pl.when(x == 3)
-    def _():
-        attend(both(right_x, 0) + both(far_x, 0))
-
-    @pl.when(x == 2)
-    def _():
-        attend(both(far_x, 0))
-
-    swap_stat.wait_recv()
-    swap_part.wait_recv()
-    other_max, other_total = stat_in[0:1, :], stat_in[1:2, :]
-    own_max, own_total = m_buf[0], acc[0, HD:HD + 1, :]
-    top = jnp.maximum(own_max, other_max)
-    own_scale = jnp.exp2((own_max - top) * SCALE)
-    other_weight = other_total * jnp.exp2((other_max - top) * SCALE)
-    denominator = own_total * own_scale + other_weight
-    mixed = (acc[0, :HD, :] * own_scale + part_in[...].astype(F32) * other_weight) / denominator
+
+    def send_part():
+        total = acc[1, HD:HD + 1, :]
+        stat_out[0:1, :] = m_buf[1]
+        stat_out[1:2, :] = total
+        stat_out[2:, :] = jnp.zeros((6, ROWS), F32)
+        swap_stat.start()
+        part_out[...] = (acc[1, :HD, :] / jnp.where(total > 0.0, total, 1.0)).astype(BF16)
+        for swap in swap_parts:
+            swap.start()
+
+    def open_phase(phase):
+        @pl.when(phase == 1)
+        def _():
+            finish(v_in, v_out)
+
+            @pl.when(x == 3)
+            def _():
+                take(right_x)
+
+            swap_early.wait_recv()
+            swap_late.wait_recv()
+            qt[1, :HD, :] = flat(qg[1]).T
+
+        @pl.when(phase == 2)
+        def _():
+            for array in (k_in, v_in):
+                wait(array, 9, 10)
+
+            @pl.when(x >= 2)
+            def _():
+                take(far_x)
+
+        @pl.when(phase == 3)
+        def _():
+            send_part()
+
+    has_left, has_right, has_far = ((x >= 1).astype(jnp.int32), (x == 3).astype(jnp.int32), (x >= 2).astype(jnp.int32))
+
+    def run_phase(phase, carry):
+        open_phase(phase)
+        side = ((phase == 1) | (phase == 2)).astype(jnp.int32)
+        skip = jnp.where(phase == 0, 1, jnp.where(phase == 1, half, jnp.where(phase == 2, 3, 3 - has_right)))
+        stop = jnp.where(phase == 0, 1 + has_left, jnp.where(phase == 1, 1 + has_left + has_right, 3 + has_far))
+
+        def run_pair(turn, inner):
+            pos = jnp.where(turn == 0, x, jnp.where(turn == 1, left_x, jnp.where(turn == 2, right_x, far_x)))
+            attend([(pos * 2 + core, side), (pos * 2 + other_core, side)])
+            return inner
+
+        return lax.fori_loop(skip, stop, run_pair, carry)
+
+    lax.fori_loop(0, 4, run_phase, 0)
     gates = gate_ref[...]
     step_id = lax.broadcasted_iota(jnp.int32, gates.shape, 0)
     gate = jnp.sum(jnp.where(step_id == step_ref[role], gates, 0.0), axis=0, keepdims=True)
-    attended = mixed.T.astype(BF16).astype(F32) * gate
-    obuf[...] = attended.reshape(PEERS, PIECE, HD).astype(BF16)
-
-    def give(turn, carry):
-        to_seq = source_of(turn)
-        pltpu.make_async_remote_copy(
-            src_ref=obuf.at[to_seq], dst_ref=out_ref.at[:, columns], send_sem=a2a_send.at[3],
-            recv_sem=a2a_recv.at[3], device_id=(role, to_seq), device_id_type=MESH,
-        ).start()
-        return carry
-
-    @pl.when(has_self == 1)
-    def _():
-        pltpu.make_async_copy(obuf.at[seq], out_ref.at[:, columns], a2a_recv.at[3]).start()
-
-    @pl.when(has_self == 0)
-    def _():
-        give(0, 0)
-
-    lax.fori_loop(1, PEERS, give, 0)
+    swap_stat.wait_recv()
+
+    def give(turn, part):
+        to_seq = lax.rem(part * 2 + lax.rem(lax.div(turn, 8) + z_lo, 2), 4) * 8 + lax.rem(y + lax.rem(turn, 8), 8)
+        here = (role == span) & (to_seq == seq)
+
+        @pl.when(here)
+        def _():
+            pltpu.make_async_copy(obuf.at[to_seq], out_ref.at[:, columns], a2a_recv.at[3, 0]).start()
+
+        @pl.when(jnp.logical_not(here))
+        def _():
+            pltpu.make_async_remote_copy(
+                src_ref=obuf.at[to_seq], dst_ref=out_ref.at[:, columns], send_sem=a2a_send.at[3],
+                recv_sem=a2a_recv.at[3, 0], device_id=(role, to_seq), device_id_type=MESH,
+            ).start()
+
+        return part
+
+    for part in range(2):
+        at = slice(part * (ROWS // 2), (part + 1) * (ROWS // 2))
+        swap_parts[part].wait_recv()
+        other_max, other_total = stat_in[0:1, at], stat_in[1:2, at]
+        own_max, own_total = m_buf[0, :, at], acc[0, HD:HD + 1, at]
+        top = jnp.maximum(own_max, other_max)
+        own_scale = jnp.exp2((own_max - top) * SCALE)
+        other_weight = other_total * jnp.exp2((other_max - top) * SCALE)
+        denominator = own_total * own_scale + other_weight
+        mixed = (acc[0, :HD, at] * own_scale + part_in[:, at].astype(F32) * other_weight) / denominator
+        attended = mixed.T.astype(BF16).astype(F32) * gate
+        obuf[part * (PEERS // 2):(part + 1) * (PEERS // 2)] = attended.reshape(PEERS // 2, PIECE, HD).astype(BF16)
+        lax.fori_loop(0, PEERS // 2, give, part)
 
     for array in (k_out, v_out):
-        for copy in array:
-            copy.wait_send()
-    for copy in (swap_queries, swap_part, swap_stat):
+        for number, copy in enumerate(array):
+            pl.when(needed[number])(copy.wait_send)
+    for copy in (swap_early, swap_late, *swap_parts, swap_stat):
         copy.wait_send()
-    whole(out_ref, a2a_recv.at[3]).wait()
-
-    @pl.when(has_self == 1)
-    def _():
-        for which in range(4):
-            whole(obuf.at[pl.ds(0, PEERS - 1)], a2a_send.at[which]).wait()
-
-    @pl.when(has_self == 0)
-    def _():
-        for which in range(4):
-            whole(obuf, a2a_send.at[which]).wait()
+    whole(out_ref, a2a_recv.at[3, 0]).wait()
+    pl.when(last)(lambda: sent(2))
+    pl.when(sends_own)(lambda: sent(0))
+    sent(3)
 
 
 def shards(queries, keys, values, step_index, frame_counts, frame_layout, gate_table):
@@ -432,11 +488,11 @@
             pltpu.VMEM((HD, ROWS), BF16),
             pltpu.VMEM((8, ROWS), F32),
             pltpu.SemaphoreType.DMA((4,)),
-            pltpu.SemaphoreType.DMA((4,)),
+            pltpu.SemaphoreType.DMA((4, 2)),
             pltpu.SemaphoreType.DMA((2, 11)),
             pltpu.SemaphoreType.DMA((2, 11)),
-            pltpu.SemaphoreType.DMA((3,)),
-            pltpu.SemaphoreType.DMA((3,)),
+            pltpu.SemaphoreType.DMA((5,)),
+            pltpu.SemaphoreType.DMA((5,)),
         ],
         compiler_params=pltpu.CompilerParams(
             collective_id=0, has_side_effects=True, vmem_limit_bytes=60 << 20

time: 61.5 us -> 60.7 us (0.987)
  Pallas kernels: 59.7 us -> 58.9 us
    pallas_call x1, Pallas kernels: 59.7 us -> 58.9 us  [shards(): pl.pallas_call(kernel, out_shape=jax.ShapeDtypeStruct(block, BF16), in_sp...]
where the time goes in v3:
time: 60.7 us; the launch traced here: 60.5 us
  Pallas kernels  58.9 us (97%)
  local copies, waits for them, and re-layouts  1.62 us (3%)
    pallas_call x1, Pallas kernels, shards(): pl.pallas_call(kernel, out_shape=jax.ShapeDtypeStruct(block, BF16), in_sp...  58.9 us
    unnamed x1, local copies, waits for them, and re-layouts  1.62 us

profile of v3, /device:TPU:6, one launch (start us, length us, event | category | flops | bytes accessed | tf_op | source)
XLA Modules:
  0.0 60.5 jit_solution(931703953896358960)
XLA Ops:
  0.0 58.9 %shard_map.73 = bf16[24,4096]{1,0:T(8,128)(2,1)} custom-call(bf16[24,4096]{1,0:T(8,128)(2,1)} %bitcast.5, bf16[24,4096]{1,0:T(8,128)(2,1)} %bitcast.6, bf16[24,4096]{1,0:T(8,128)(2,1)} %bitcast.7, s32[16]{0:T(128)} %step_hbm.1, s32[16]{0:T(128)} %count_hbm.1, s32[8,8]{1,0:T(8,128)} %layout_hbm.1, f32[16,4096]{1,0:T(8,128)} %gate_hbm.1), custom_call_target="tpu_custom_call" | custom-call | tf_op jit(solution)/shard_map/pallas_call | solution.py:462
  58.9 1.6 %copy.9 = bf16[1,24,4096]{2,1,0:T(8,128)(2,1)} copy(bf16[1,24,4096]{2,1,0:T(8,128)(2,1)} %bitcast.4) | data formatting | bytes 393216

commit v4 on v3

--- a/solution.py
+++ b/solution.py
@@ -255,10 +255,11 @@
     sib = x * 2 + other_core
 
     last = x == 3
-    sends_own, has_left_item, has_right_item, has_far_item = x != 3, x != 0, x != 2, x != 1
+    sends_own = x != 3
     always = x >= 0
-    needed = (sends_own,) * 4 + (always, has_left_item, has_right_item, has_left_item, has_right_item, has_far_item, has_far_item)
-    expected = (has_left_item,) * 2 + (has_right_item,) * 2 + (always, has_far_item, has_far_item) + needed[7:]
+    ends, middle, later = (x == 0) | last, (x == 1) | (x == 2), x >= 2
+    needed = (sends_own, sends_own, x <= 1, x == 0, always, middle, ends, x >= 1, last, later, later)
+    expected = (x >= 1, x >= 1, ends, last, always, later, later, x >= 1, last, later, later)
 
     def start(copies, *numbers):
         for number in numbers:
@@ -366,48 +367,33 @@
         for swap in swap_parts:
             swap.start()
 
-    def open_phase(phase):
-        @pl.when(phase == 1)
-        def _():
-            finish(v_in, v_out)
-
-            @pl.when(x == 3)
-            def _():
-                take(right_x)
-
-            swap_early.wait_recv()
-            swap_late.wait_recv()
-            qt[1, :HD, :] = flat(qg[1]).T
-
-        @pl.when(phase == 2)
-        def _():
-            for array in (k_in, v_in):
-                wait(array, 9, 10)
-
-            @pl.when(x >= 2)
-            def _():
-                take(far_x)
-
-        @pl.when(phase == 3)
-        def _():
-            send_part()
-
-    has_left, has_right, has_far = ((x >= 1).astype(jnp.int32), (x == 3).astype(jnp.int32), (x >= 2).astype(jnp.int32))
-
-    def run_phase(phase, carry):
-        open_phase(phase)
-        side = ((phase == 1) | (phase == 2)).astype(jnp.int32)
-        skip = jnp.where(phase == 0, 1, jnp.where(phase == 1, half, jnp.where(phase == 2, 3, 3 - has_right)))
-        stop = jnp.where(phase == 0, 1 + has_left, jnp.where(phase == 1, 1 + has_left + has_right, 3 + has_far))
-
-        def run_pair(turn, inner):
-            pos = jnp.where(turn == 0, x, jnp.where(turn == 1, left_x, jnp.where(turn == 2, right_x, far_x)))
-            attend([(pos * 2 + core, side), (pos * 2 + other_core, side)])
-            return inner
-
-        return lax.fori_loop(skip, stop, run_pair, carry)
-
-    lax.fori_loop(0, 4, run_phase, 0)
+    def both(pos, side):
+        return [(pos * 2 + core, side), (pos * 2 + other_core, side)]
+
+    @pl.when(x >= 1)
+    def _():
+        attend(both(left_x, 0))
+
+    finish(v_in, v_out)
+    pl.when(last)(lambda: take(right_x))
+    swap_early.wait_recv()
+    swap_late.wait_recv()
+    qt[1, :HD, :] = flat(qg[1]).T
+    pl.when(half == 0)(lambda: attend(both(x, 1)))
+    pl.when(middle)(lambda: attend(both(left_x, 1)))
+    pl.when(last)(lambda: attend(both(left_x, 1) + both(right_x, 1)))
+    for array in (k_in, v_in):
+        wait(array, 9, 10)
+
+    @pl.when(later)
+    def _():
+        take(far_x)
+        attend(both(far_x, 1))
+
+    send_part()
+    pl.when(last)(lambda: attend(both(right_x, 0) + both(far_x, 0)))
+    pl.when(x == 2)(lambda: attend(both(far_x, 0)))
+
     gates = gate_ref[...]
     step_id = lax.broadcasted_iota(jnp.int32, gates.shape, 0)
     gate = jnp.sum(jnp.where(step_id == step_ref[role], gates, 0.0), axis=0, keepdims=True)

time: 60.7 us -> 60.1 us (level)
  no operation moved by 1% of the time
where the time goes in v4:
time: 60.1 us; the launch traced here: 60 us
  Pallas kernels  58.4 us (97%)
  local copies, waits for them, and re-layouts  1.62 us (3%)
    pallas_call x1, Pallas kernels, shards(): pl.pallas_call(kernel, out_shape=jax.ShapeDtypeStruct(block, BF16), in_sp...  58.4 us
    unnamed x1, local copies, waits for them, and re-layouts  1.62 us

profile of v4, /device:TPU:6, one launch (start us, length us, event | category | flops | bytes accessed | tf_op | source)
XLA Modules:
  0.0 60.0 jit_solution(9630911603843173651)
XLA Ops:
  0.0 58.4 %shard_map.73 = bf16[24,4096]{1,0:T(8,128)(2,1)} custom-call(bf16[24,4096]{1,0:T(8,128)(2,1)} %bitcast.5, bf16[24,4096]{1,0:T(8,128)(2,1)} %bitcast.6, bf16[24,4096]{1,0:T(8,128)(2,1)} %bitcast.7, s32[16]{0:T(128)} %step_hbm.1, s32[16]{0:T(128)} %count_hbm.1, s32[8,8]{1,0:T(8,128)} %layout_hbm.1, f32[16,4096]{1,0:T(8,128)} %gate_hbm.1), custom_call_target="tpu_custom_call" | custom-call | tf_op jit(solution)/shard_map/pallas_call | solution.py:448
  58.4 1.6 %copy.9 = bf16[1,24,4096]{2,1,0:T(8,128)(2,1)} copy(bf16[1,24,4096]{2,1,0:T(8,128)(2,1)} %bitcast.4) | data formatting | bytes 393216
